TPU v7x, 32 devices: a whole 2x2x4 slice. The times are simulated.
32 devices in a mesh: seq: 8 (over z, y), tensor: 4 (over x, core).
Axes of the slice: x: 2, y: 2, z: 4, core: 2. Of those that a mesh axis runs over, the one named last changes fastest.
Arguments:
- state: bfloat16 [8192, 2048], P('seq', 'tensor'), may hold values from -20.5 to 20.5
- memory: bfloat16 [128, 2048], P('seq', 'tensor'), may hold values from -20.5 to 20.5
- w_query: bfloat16 [2048, 2048], P('seq', 'tensor'), may hold values from -0.1875 to 0.1875
- w_key: bfloat16 [2048, 2048], P('seq', 'tensor'), may hold values from -0.1875 to 0.1875
- w_value: bfloat16 [2048, 2048], P('seq', 'tensor'), may hold values from -0.125 to 0.125
- w_output: bfloat16 [2048, 2048], P('tensor', 'seq'), may hold values from -0.375 to 0.375
- norm_gain: float32 [2048], P('tensor'), may hold values from 0.1 to 1.9
- remaining: int32 [8192], P('seq'), may hold values from 0 to 3
- slot_home: int32 [128], replicated, may hold values from 0 to 7
Outputs:
- new_state: bfloat16 [8192, 2048], P('seq', 'tensor')
- new_memory: bfloat16 [128, 2048], P('seq', 'tensor')
Inputs may be any that keep to these rules, and one draw needn't show every extreme that they name: `remaining`: 0 means the token has halted.
All inputs are finite; a program needn't handle non-finite values.
Results may differ from a plain program's by a relative error of at most 0.014.
The roundings to bfloat16 on the way count: a program that leaves them out, or rounds other values in their place, can miss the bound.
Values may be sent and summed in bfloat16 or wider, within the bound.
A program may use at most 128 MiB of HBM per device.

v0:
```python
import math

import jax
import jax.numpy as jnp
from jax import lax
from jax.sharding import PartitionSpec as P

D = 2048
H = 16
HD = 128
HALF = 256
QB = 512


EPS = 1e-05
MASKED = -1e30


def with_halo(array, sides, width):
    for axis, dim in sides:
        peers, length = (lax.axis_size(axis), array.shape[dim])
        up = [(i, (i + 1) % peers) for i in range(peers - 1)]
        down = [(j, i) for i, j in up]
        last = lax.slice_in_dim(array, length - width, length, axis=dim)
        initial = lax.slice_in_dim(array, 0, width, axis=dim)
        before = lax.ppermute(last, axis, up)
        after = lax.ppermute(initial, axis, down)
        array = jnp.concatenate([before, array, after], axis=dim)
    return array


def merged(part, axis, combine):
    gathered = jax.tree.map(lambda a: lax.all_gather(a, axis), part)

    def take(source):
        return jax.tree.map(lambda a: lax.dynamic_index_in_dim(a, source, 0, False), gathered)

    return lax.fori_loop(
        1, lax.axis_size(axis), lambda source, state: combine(state, take(source)), take(0)
    )


def head_slopes(first, amount):
    order = (first + jnp.arange(amount, dtype=jnp.int32)).astype(jnp.float32)
    return 0.25 * 8.0 ** (order / (H - 1))


def shards(state, memory, w_query, w_key, w_value, w_output, norm_gain, remaining, slot_home):
    tok_rows = state.shape[0]
    slot_rows = memory.shape[0]
    seq_count = lax.axis_size("seq")
    seq_place = lax.axis_index("seq")
    tensor_place = lax.axis_index("tensor")
    local_width = w_query.shape[1]
    local_heads = local_width // HD
    total_tokens = tok_rows * seq_count
    score_scale = 1.0 / math.sqrt(HD)
    distance_slopes = head_slopes(tensor_place * local_heads, local_heads)
    homes = slot_home.astype(jnp.float32)
    home_gap = jnp.abs(homes - seq_place.astype(jnp.float32))
    slot_bias = distance_slopes[:, None] * home_gap[None, :]
    state_full, memory_full = (
        lax.all_gather(state, "tensor", axis=1, tiled=True),
        lax.all_gather(memory, "tensor", axis=1, tiled=True),
    )
    memory_every = lax.all_gather(memory_full, "seq", axis=0, tiled=True)
    rows_full = jnp.concatenate([state_full, memory_every], axis=0)
    pieces = (
        lax.all_gather(w_query, "seq", axis=0, tiled=True),
        lax.all_gather(w_key, "seq", axis=0, tiled=True),
        lax.all_gather(w_value, "seq", axis=0, tiled=True),
    )
    query_acc, key_acc, value_acc = tuple(
        (jnp.dot(rows_full, piece, preferred_element_type=jnp.float32) for piece in pieces)
    )
    query = query_acc.astype(jnp.bfloat16)
    keys = key_acc.astype(jnp.bfloat16)
    values = value_acc.astype(jnp.bfloat16)
    memory_slot_query = query[tok_rows:].reshape(-1, local_heads, HD)
    memory_slot_keys = keys[tok_rows:].reshape(-1, local_heads, HD)
    memory_slot_values = values[tok_rows:].reshape(-1, local_heads, HD)
    token_key_rows = keys[:tok_rows].reshape(tok_rows, local_heads, HD)
    token_value_rows = values[:tok_rows].reshape(tok_rows, local_heads, HD)
    keys_values = jnp.concatenate([keys[:tok_rows], values[:tok_rows]], axis=1)
    padded = with_halo(keys_values, (("seq", 0),), HALF)
    block = QB
    window_extent = block + 2 * HALF

    def one_block(number):
        start = number * block
        query_matrix = lax.dynamic_slice_in_dim(query, start, block, 0).reshape(
            block, local_heads, HD
        )
        near_rows = lax.dynamic_slice_in_dim(padded, start, window_extent, 0)
        near_keys = near_rows[:, :local_width].reshape(window_extent, local_heads, HD)
        near_values = near_rows[:, local_width:].reshape(window_extent, local_heads, HD)
        near = (
            jnp.einsum("qhd,khd->hqk", query_matrix, near_keys, preferred_element_type=jnp.float32)
            * score_scale
        )
        first = seq_place * tok_rows + start
        qpos = first + jnp.arange(block, dtype=jnp.int32)
        kpos = first - HALF + jnp.arange(window_extent, dtype=jnp.int32)
        valid = (
            (jnp.abs(qpos[:, None] - kpos[None, :]) <= HALF)
            & (kpos >= 0)[None, :]
            & (kpos < total_tokens)[None, :]
        )
        near = jnp.where(valid[None], near, MASKED)
        distant_mask = (
            jnp.einsum(
                "taw,caw->atc", query_matrix, memory_slot_keys, preferred_element_type=jnp.float32
            )
            * score_scale
            - slot_bias[:, None, :]
        )
        scores = jnp.concatenate([near, distant_mask], axis=2)
        top = jnp.max(scores, axis=2, keepdims=True)
        exponent_terms = jnp.exp(scores - top)
        total = jnp.sum(exponent_terms, axis=2)
        attention_probabilities = exponent_terms.astype(jnp.bfloat16)
        numer = jnp.einsum(
            "hqk,khd->qhd",
            attention_probabilities[:, :, :window_extent],
            near_values,
            preferred_element_type=jnp.float32,
        )
        numer = numer + jnp.einsum(
            "lse,elf->slf",
            attention_probabilities[:, :, window_extent:],
            memory_slot_values,
            preferred_element_type=jnp.float32,
        )
        return (
            (numer / jnp.transpose(total)[:, :, None])
            .astype(jnp.bfloat16)
            .reshape(block, local_width)
        )

    token_mix = lax.map(one_block, jnp.arange(tok_rows // block, dtype=jnp.int32)).reshape(
        tok_rows, local_width
    )
    unnormalized_scores = (
        jnp.einsum(
            "gki,pki->kgp", memory_slot_query, token_key_rows, preferred_element_type=jnp.float32
        )
        * score_scale
        - slot_bias[:, :, None]
    )
    local_top = jnp.max(unnormalized_scores, axis=2)
    exponent_terms = jnp.exp(unnormalized_scores - local_top[:, :, None])
    local_sum = jnp.transpose(jnp.sum(exponent_terms, axis=2))
    local_num = jnp.einsum(
        "xzg,gxw->zxw",
        exponent_terms.astype(jnp.bfloat16),
        token_value_rows,
        preferred_element_type=jnp.float32,
    )
    local_top = jnp.transpose(local_top)

    def combine(first_part, second_part):
        top = jnp.maximum(first_part[0], second_part[0])
        weight_first = jnp.exp(first_part[0] - top)
        weight_second = jnp.exp(second_part[0] - top)
        sums = weight_first * first_part[1] + weight_second * second_part[1]
        numers = (
            weight_first[:, :, None] * first_part[2] + weight_second[:, :, None] * second_part[2]
        )
        return (top, sums, numers)

    merged_parts = merged((local_top, local_sum, local_num), "seq", combine)
    own_sum = lax.dynamic_slice_in_dim(merged_parts[1], seq_place * slot_rows, slot_rows, 0)
    own_num = lax.dynamic_slice_in_dim(merged_parts[2], seq_place * slot_rows, slot_rows, 0)
    slot_mix = (own_num / own_sum[:, :, None]).astype(jnp.bfloat16).reshape(slot_rows, local_width)
    mixed = jnp.concatenate([token_mix, slot_mix], axis=0)
    partial_rows = jnp.dot(
        mixed,
        lax.all_gather(w_output, "seq", axis=1, tiled=True),
        preferred_element_type=jnp.float32,
    )
    summed = lax.psum_scatter(
        partial_rows.astype(jnp.bfloat16), "tensor", scatter_dimension=1, tiled=True
    ).astype(jnp.float32)
    residual = jnp.concatenate([state, memory], axis=0).astype(jnp.float32) + summed
    squares = lax.psum(jnp.sum(residual * residual, axis=1), "tensor")
    normed_rows = (residual * lax.rsqrt(squares / D + EPS)[:, None] * norm_gain[None, :]).astype(
        jnp.bfloat16
    )
    new_state = jnp.where((remaining > 0)[:, None], normed_rows[:tok_rows], state)
    new_memory = normed_rows[tok_rows:]
    return (new_state, new_memory)


def solution(mesh):
    placed = (
        P("seq", "tensor"),
        P("seq", "tensor"),
        P("seq", "tensor"),
        P("seq", "tensor"),
        P("seq", "tensor"),
        P("tensor", "seq"),
        P("tensor"),
        P("seq"),
        P(),
    )
    return jax.shard_map(
        shards,
        mesh=mesh,
        in_specs=placed,
        out_specs=(P("seq", "tensor"), P("seq", "tensor")),
        check_vma=False,
    )
```

profile of v0, /device:TPU:0, one launch (start us, length us, event | category | flops | bytes accessed | tf_op | source)
XLA Modules:
  0.0 395.7 jit_solution(2981081601657739276)
XLA Ops:
  10.0 6.4 %all_gather.40 = bf16[16,2048]{1,0:T(8,128)(2,1)S(1)} all-gather(bf16[16,512]{1,0:T(8,128)(2,1)} %param.14), channel_id=1, replica_groups=mesh['seq'=8,'tensor'=4] {'tensor'}, dimensions={1}, use_global_device_ids=true | all-gather | bytes 81920 | tf_op jit(solution)/shard_map/all_gather | solution.py:64
  17.2 32.4 %all_gather.41 = bf16[128,2048]{1,0:T(8,128)(2,1)S(1)} all-gather(bf16[16,2048]{1,0:T(8,128)(2,1)S(1)} %all_gather.40), channel_id=1, replica_groups=mesh['seq'=8,'tensor'=4] {'seq'}, dimensions={0}, use_global_device_ids=true | all-gather | bytes 589824 | tf_op jit(solution)/shard_map/all_gather | solution.py:66
  49.5 4.7 %constant_dynamic-update-slice_fusion.2 = bf16[1152,2048]{1,0:T(8,128)(2,1)} fusion(bf16[1024,2048]{1,0:T(8,128)(2,1)} %all-gather.10.cloned.1.call-done), kind=kLoop, calls=%fused_computation.64 | loop fusion | bytes 8388608
  54.3 0.8 constant_dynamic-update-slice_fusion.1
  55.1 43.1 %all-gather.12.cloned.1.call-done = bf16[2048,512]{1,0:T(8,128)(2,1)} async-done(((bf16[256,512]{1,0:T(8,128)(2,1)}), bf16[2048,512]{1,0:T(8,128)(2,1)}) %all-gather.12.cloned.1.call-update) | async-done | bytes 2097168 | tf_op jit(solution)/shard_map/all_gather | solution.py:70
  98.2 6.0 %convolution_convert_fusion.3 = bf16[1152,512]{0,1:T(8,128)(2,1)S(1)} fusion(bf16[1152,2048]{1,0:T(8,128)(2,1)} %constant_dynamic-update-slice_fusion.1, bf16[2048,512]{1,0:T(8,128)(2,1)} %all-gather.12.cloned.1.call-done), kind=kOutput, calls=%fused_computation.39 | convolution fusion | flops 2416508928 | bytes 7995392 | tf_op jit(solution)/shard_map/dot_general | solution.py:74
  104.3 43.8 %all-gather.16.cloned.1.call-done = bf16[2048,512]{1,0:T(8,128)(2,1)} async-done(((bf16[256,512]{1,0:T(8,128)(2,1)}), bf16[2048,512]{1,0:T(8,128)(2,1)}) %all-gather.16.cloned.1.call-update) | async-done | bytes 2097168 | tf_op jit(solution)/shard_map/all_gather | solution.py:69
  148.2 6.0 %convolution_convert_fusion.1 = bf16[1152,512]{0,1:T(8,128)(2,1)S(1)} fusion(bf16[1152,2048]{1,0:T(8,128)(2,1)} %constant_dynamic-update-slice_fusion.1, bf16[2048,512]{1,0:T(8,128)(2,1)} %all-gather.16.cloned.1.call-done), kind=kOutput, calls=%fused_computation.37 | convolution fusion | flops 2416508928 | bytes 7995392 | tf_op jit(solution)/shard_map/dot_general | solution.py:74
  154.1 1.1 copy-done.2
  155.3 42.7 %all-gather.14.cloned.1.call-done = bf16[2048,512]{1,0:T(8,128)(2,1)} async-done(((bf16[256,512]{1,0:T(8,128)(2,1)}), bf16[2048,512]{1,0:T(8,128)(2,1)}) %all-gather.14.cloned.1.call-update) | async-done | bytes 2097168 | tf_op jit(solution)/shard_map/all_gather | solution.py:71
  198.0 6.0 %convolution_convert_fusion.2 = bf16[1152,512]{0,1:T(8,128)(2,1)S(1)} fusion(bf16[1152,2048]{1,0:T(8,128)(2,1)} %constant_dynamic-update-slice_fusion.1, bf16[2048,512]{1,0:T(8,128)(2,1)} %all-gather.14.cloned.1.call-done), kind=kOutput, calls=%fused_computation.38 | convolution fusion | flops 2416508928 | bytes 7995392 | tf_op jit(solution)/shard_map/dot_general | solution.py:74
  205.0 1.3 copy-done.1
  206.3 1.5 convolution_bitcast_fusion.1
  207.9 1.1 pad_maximum_fusion.3
  208.9 3.3 collective-permute-start
  212.2 1.3 collective-permute-start.1
  213.6 2.3 fusion.24
  215.9 43.2 %all-gather.1 = f32[1024,4]{0,1:T(4,128)S(1)} all-gather(f32[128,4]{0,1:T(4,128)S(1)} %bitcast.113), channel_id=3, replica_groups=mesh['seq'=8,'tensor'=4] {'seq'}, dimensions={0}, use_global_device_ids=true | all-gather | bytes 18432 | tf_op jit(solution)/shard_map/all_gather | solution.py:33
  259.0 26.1 %all-gather = f32[1024,4]{0,1:T(4,128)S(1)} all-gather(f32[128,4]{0,1:T(4,128)S(1)} %bitcast.111), channel_id=2, replica_groups=mesh['seq'=8,'tensor'=4] {'seq'}, dimensions={0}, use_global_device_ids=true | all-gather | bytes 18432 | tf_op jit(solution)/shard_map/all_gather | solution.py:33
  285.3 7.8 %pad_maximum_fusion = bf16[1536,1024]{0,1:T(8,128)(2,1)} fusion(bf16[256,1024]{0,1:T(8,128)(2,1)} %collective-permute-done.1, bf16[1024,512]{0,1:T(8,128)(2,1)S(1)} %slice.75, bf16[1024,512]{0,1:T(8,128)(2,1)S(1)} %slice.74, bf16[256,1024]{0,1:T(8,128)(2,1)} %collective-permute-done), kind=kLoop, calls=%fused_computation.36 | loop fusion | flops 12582912 | bytes 6291456 | tf_op jit(solution)/shard_map/concatenate | solution.py:28
  293.2 26.1 %while.33 = (s32[]{:T(128)}, bf16[2,512,512]{2,1,0:T(8,128)(2,1)}, s32[2]{0:T(128)S(1)}, bf16[1536,1024]{0,1:T(8,128)(2,1)}, s32[]{:T(128)}, /*index=5*/bf16[115...) while((s32[]{:T(128)}, bf16[2,512,512]{2,1,0:T(8,128)(2,1)}, ...), condition=%wide.region_4.5_spmd.clone, body=%wide.region_0.4_spmd.clone.sunk | while | flops 1227883520 | bytes 51204984 | solution.py:140
  295.2 1.7 constant_dynamic-slice_fusion.5
  297.0 1.1 constant_dynamic-slice_fusion.6
  298.1 1.9 fusion.84
  300.6 1.8 fusion.85
  302.5 1.5 fusion.86
  305.3 1.0 copy-done.10
  308.3 1.7 constant_dynamic-slice_fusion.5
  310.0 1.1 constant_dynamic-slice_fusion.6
  311.1 1.9 fusion.84
  313.7 1.8 fusion.85
  315.5 1.5 fusion.86
  318.3 1.0 copy-done.10
  319.3 1.0 slice.81
  320.4 2.0 copy.40
  322.4 7.4 %while.32 = (s32[]{:T(128)}, f32[128,4]{0,1:T(4,128)S(1)}, f32[128,4]{0,1:T(4,128)S(1)}, f32[128,4,128]{2,1,0:T(4,128)S(1)}, f32[8,128,4]{1,2,0:T(4,128)S(1)}, /...) while((s32[]{:T(128)}, f32[128,4]{0,1:T(4,128)S(1)}, ...), condition=%wide.region_8.9_spmd, body=%wide.region_7.8_spmd.sunk | while | flops 199685 | bytes 815255 | solution.py:38
  322.7 0.8 fusion.72
  323.8 0.8 fusion.72
  324.8 0.8 fusion.72
  325.9 0.8 fusion.72
  327.0 0.8 fusion.72
  328.0 0.8 fusion.72
  329.1 0.8 fusion.72
  330.2 6.3 %convolution_convert_fusion = bf16[1040,2048]{1,0:T(8,128)(2,1)} fusion(bf16[512,2048]{1,0:T(8,128)(2,1)} %all-gather.18.cloned.1.call-done, bf16[16,512]{1,0:T(8,128)(2,1)S(1)} %bitcast.112, bf16[1024,512]{1,0:T(8,128)(2,1)} %bitcast.114), kind=kOutput, calls=%fused_computation.35 | convolution fusion | flops 2185297920 | bytes 7421952 | tf_op jit(solution)/shard_map/dot_general | solution.py:176
  337.2 41.8 %reduce-scatter.2.cloned.1.call-done = bf16[1040,512]{1,0:T(8,128)(2,1)} async-done(((bf16[1040,2048]{1,0:T(8,128)(2,1)}), bf16[1040,512]{1,0:T(8,128)(2,1)}) %reduce-scatter.2.cloned.1.call-update) | async-done | bytes 1064976 | tf_op jit(solution)/shard_map/reduce_scatter | solution.py:181
  379.0 1.8 multiply_reduce_fusion
  380.7 5.9 %psum.7 = f32[1040]{0:T(1024)S(1)} all-reduce(f32[1040]{0:T(1024)S(1)} %multiply_reduce_fusion), channel_id=1, replica_groups=mesh['seq'=8,'tensor'=4] {'tensor'}, use_global_device_ids=true, to_apply=%region_11.12 | all-reduce | flops 1040 | bytes 8320 | tf_op jit(solution)/shard_map/psum | solution.py:185
  387.6 1.2 slice_select_fusion
  (109 shorter events, 15.5 us)
Async XLA Ops:
  7.2 42.4 %all-gather.10.cloned.1.call-start = ((), (), s32[]{:S(2)}) async-start(), calls=%async_computation.1 | async-start | bytes 5242880 | tf_op jit(solution)/shard_map/all_gather | solution.py:63
  7.9 90.3 %all-gather.12.cloned.1.call-start = ((), (), s32[]{:S(2)}) async-start(), calls=%async_computation.2 | async-start | bytes 2359296 | tf_op jit(solution)/shard_map/all_gather | solution.py:70
  8.6 139.5 %all-gather.16.cloned.1.call-start = ((), (), s32[]{:S(2)}) async-start(), calls=%async_computation.4 | async-start | bytes 2359296 | tf_op jit(solution)/shard_map/all_gather | solution.py:69
  9.4 188.6 %all-gather.14.cloned.1.call-start = ((), (), s32[]{:S(2)}) async-start(), calls=%async_computation.3 | async-start | bytes 2359296 | tf_op jit(solution)/shard_map/all_gather | solution.py:71
  10.0 309.3 %all-gather.20.cloned.1.call-start = ((), (), s32[]{:S(2)}) async-start(), calls=%async_computation.7 | async-start | bytes 2359296 | tf_op jit(solution)/shard_map/all_gather | solution.py:33
  104.2 109.4 %copy-start.4 = (bf16[1152,512]{0,1:T(8,128)(2,1)}, bf16[1152,512]{0,1:T(8,128)(2,1)S(1)}, u32[]{:S(2)}) copy-start(bf16[1152,512]{0,1:T(8,128)(2,1)S(1)} %convolution_convert_fusion.3) | copy-start | bytes 3538948
  154.1 1.1 copy-start.2
  203.9 1.1 copy-start.5
  205.0 1.3 copy-start.1
  207.8 122.4 %all-gather.18.cloned.1.call-start = ((), (), s32[]{:S(2)}) async-start(), calls=%async_computation.5 | async-start | bytes 2359296 | tf_op jit(solution)/shard_map/all_gather | solution.py:178
  208.9 76.4 %collective-permute-start = (bf16[256,1024]{0,1:T(8,128)(2,1)}, bf16[256,1024]{0,1:T(8,128)(2,1)}, u32[]{:S(2)}, u32[]{:S(2)}) collective-permute-start(bf16[256,1024]{0,1:T(8,128)(2,1)} %get-tuple-element.403), channel_id=1, source_target_pairs={{0,4},{4,8},{8,12},{12,16},{16,20},{20,24},{24,28},{1,5},{5,9},{9,... | collective-permute-start | bytes 1572872 | tf_op jit(solution)/shard_map/ppermute | solution.py:26
  212.2 73.1 %collective-permute-start.1 = (bf16[256,1024]{0,1:T(8,128)(2,1)}, bf16[256,1024]{0,1:T(8,128)(2,1)}, u32[]{:S(2)}, u32[]{:S(2)}) collective-permute-start(bf16[256,1024]{0,1:T(8,128)(2,1)} %get-tuple-element.404), channel_id=1, source_target_pairs={{4,0},{8,4},{12,8},{16,12},{20,16},{24,20},{28,24},{5,1},{9,5},{13... | collective-permute-start | bytes 1572872 | tf_op jit(solution)/shard_map/ppermute | solution.py:27
  213.5 165.5 %reduce-scatter.2.cloned.1.call-start = ((), (), s32[]{:S(2)}) async-start(), calls=%async_computation.6 | async-start | bytes 5324800 | tf_op jit(solution)/shard_map/reduce_scatter | solution.py:181
  213.6 71.6 %slice-start = ((bf16[1152,512]{0,1:T(8,128)(2,1)}), bf16[128,512]{0,1:T(8,128)(2,1)S(1)}, s32[]{:S(2)}) async-start(bf16[1152,512]{0,1:T(8,128)(2,1)} %copy-done.4), calls=%async_computation.8 | async-start | bytes 262144 | tf_op jit(solution)/shard_map/slice | solution.py:80
  285.3 7.9 %slice-start.1 = ((bf16[1152,512]{0,1:T(8,128)(2,1)}), bf16[128,512]{0,1:T(8,128)(2,1)S(1)}, s32[]{:S(2)}) async-start(bf16[1152,512]{0,1:T(8,128)(2,1)} %copy-done.5), calls=%async_computation.9 | async-start | bytes 262144 | tf_op jit(solution)/shard_map/slice | solution.py:81
  304.0 1.2 copy-start.9
  305.2 1.0 copy-start.10
  317.0 1.2 copy-start.9
  318.3 1.0 copy-start.10
  336.5 0.7 copy-start.7
  336.5 42.5 %copy-start = (bf16[1024,512]{1,0:T(8,128)(2,1)S(1)}, bf16[1024,512]{1,0:T(8,128)(2,1)}, u32[]{:S(2)}) copy-start(bf16[1024,512]{1,0:T(8,128)(2,1)} %param.13) | copy-start | bytes 3145732
  336.5 42.5 %copy-start.6 = (bf16[16,512]{1,0:T(8,128)(2,1)S(1)}, bf16[16,512]{1,0:T(8,128)(2,1)}, u32[]{:S(2)}) copy-start(bf16[16,512]{1,0:T(8,128)(2,1)} %param.14) | copy-start | bytes 49156
  337.1 49.5 %copy-start.8 = (f32[512]{0:T(512)S(1)}, f32[512]{0:T(512)}, u32[]{:S(2)}) copy-start(f32[512]{0:T(512)} %param.19) | copy-start | bytes 6148
  379.0 7.6 %copy-start.3 = (bf16[1040,512]{1,0:T(8,128)(2,1)S(1)}, bf16[1040,512]{1,0:T(8,128)(2,1)}, u32[]{:S(2)}) copy-start(bf16[1040,512]{1,0:T(8,128)(2,1)} %reduce-scatter.2.cloned.1.call-done) | copy-start | bytes 3194884
Sparse Core Ops, SparseCore 0:
  9.6 37.1 all-gather.9
  48.9 49.2 all-gather.11
  100.4 47.7 all-gather.15
  150.1 47.7 all-gather.13
  207.9 63.3 all-gather.19
  273.3 49.3 all-gather.17
  336.6 42.3 reduce-scatter.1
where the time goes:
time: 396 us
  waiting for transfers between devices  174 us (44%)
  blocking collectives  114 us (29%)
  matrix products  34.8 us (9%)
  other arithmetic  26.5 us (7%)
  local copies, waits for them, and re-layouts  25.6 us (6%)
  between operations  14.3 us (4%)
  starting transfers between devices  4.83 us (1%)
    all_gather x2, blocking collectives, merged(): gathered = jax.tree.map(lambda a: lax.all_gather(a, axis), part)  69.3 us
    all_gather x1, waiting for transfers between devices, shards(): lax.all_gather(w_query, 'seq', axis=0, tiled=True)  43.8 us
    all_gather x1, waiting for transfers between devices, shards(): lax.all_gather(w_key, 'seq', axis=0, tiled=True)  43.1 us
    all_gather x1, waiting for transfers between devices, shards(): lax.all_gather(w_value, 'seq', axis=0, tiled=True)  42.7 us
    reduce_scatter x1, waiting for transfers between devices, shards(): lax.psum_scatter(partial_rows.astype(jnp.bfloat16), 'tensor', scatter_dim...  41.8 us
    all_gather x1, blocking collectives, shards(): memory_every = lax.all_gather(memory_full, 'seq', axis=0, tiled=True)  32.4 us
    dot_general x3, matrix products, shards(): jnp.dot(rows_full, piece, preferred_element_type=jnp.float32)  17.9 us
    unnamed x21, local copies, waits for them, and re-layouts  8.32 us
  transfers between devices with their start and end apart: 9, of which 4 were waited for; matrix products, arithmetic and copies ran while one was open for 16% of the time, Pallas kernels for 0%

commit v1 on v0

v1 whole, which is shorter than its diff:
```python
import functools
import math

import jax
import jax.numpy as jnp
from jax import lax
from jax.experimental import pallas as pl
from jax.experimental.pallas import tpu as pltpu
from jax.sharding import PartitionSpec as P

H = 16
HD = 128
HALF = 256
EPS = 1e-05
MASKED = -1e30
F32 = jnp.float32
BF16 = jnp.bfloat16
CHUNK = 256


def kernel(
    n_seq, n_tensor,
    state, memory, wq, wk, wv, wo, gain, remaining, homes,
    new_state, new_memory,
    rows, wqkv, wob, q, k, v, mask, mixed,
    num, stat, numr, statr,
    tosend, pr, own, xsend, xr, res, sqs, sqr, sqms, sqmr,
    w_send, w_recv, s_send, s_recv, h_send, h_recv, m_send, m_recv, l_sem,
    p_send, p_recv, c_send, c_recv, x_send, x_recv, q_send, q_recv,
):
    tok, width = state.shape
    srows = memory.shape[0]
    slots = homes.shape[1]
    heads = width // HD
    D = rows.shape[1]
    depth = wq.shape[0]
    bw = wo.shape[1]
    outer, X = n_seq // 2, n_tensor // 2
    nch = tok // CHUNK
    s = lax.axis_index("seq")
    t = lax.axis_index("tensor")
    o, i = s // 2, s % 2
    x, c = t // 2, t % 2
    mate = x * 2 + 1 - c
    scale = 1.0 / math.sqrt(HD)
    base_slot = HALF + tok + HALF

    def remote(src, dst, ss, rs, seq, ten):
        return pltpu.make_async_remote_copy(
            src_ref=src, dst_ref=dst, send_sem=ss, recv_sem=rs,
            device_id=(seq, ten), device_id_type=pl.DeviceIdType.MESH,
        )

    barrier = pltpu.get_barrier_semaphore()
    for d in range(1, n_seq):
        pl.semaphore_signal(barrier, inc=1, device_id=((s + d) % n_seq, t), device_id_type=pl.DeviceIdType.MESH)
    for d in range(1, n_tensor):
        pl.semaphore_signal(barrier, inc=1, device_id=(s, (t + d) % n_tensor), device_id_type=pl.DeviceIdType.MESH)
    pl.semaphore_wait(barrier, n_seq + n_tensor - 2)

    cols = pl.ds(pl.multiple_of(t * width, width), width)

    pieces = [(HALF + p * CHUNK, CHUNK) for p in range(nch)]
    pieces += [(0, HALF), (HALF + tok, HALF), (base_slot, slots)]
    BEFORE, AFTER, SLOTS = nch, nch + 1, nch + 2

    def piece_on(p):
        if p == BEFORE:
            return s > 0
        if p == AFTER:
            return s < n_seq - 1
        return None

    def when(cond, f):
        if cond is None:
            f()
        else:
            pl.when(cond)(f)

    def piece_ref(p, who):
        start, size = pieces[p]
        return rows.at[pl.ds(start, size), pl.ds(pl.multiple_of(who * width, width), width)]

    def piece_copy(p, owner, lane, seq_to_ten):
        ref = piece_ref(p, owner)
        return remote(ref, ref, s_send.at[p, lane], s_recv.at[p, owner], s, seq_to_ten)

    def piece_out(p):
        def go():
            for d in range(1, X):
                piece_copy(p, t, d, ((x + d) % X) * 2 + c).start()
            piece_copy(p, t, 0, mate).start()
        when(piece_on(p), go)

    def piece_forward(p):
        def go():
            for d in range(1, X):
                owner = ((x + X - d) % X) * 2 + c
                piece_copy(p, owner, 0, mate).wait_recv()
                piece_copy(p, owner, X - 1 + d, mate).start()
        when(piece_on(p), go)

    def piece_in(p):
        def go():
            for d in range(X):
                piece_copy(p, ((x + d) % X) * 2 + 1 - c, 0, mate).wait_recv()
        when(piece_on(p), go)

    def piece_end(p):
        def go():
            for lane in range(2 * X - 1):
                piece_copy(p, t, lane, mate).wait_send()
        when(piece_on(p), go)

    def w_own(w):
        return (wk, wv, wq, wo)[w]

    def w_ref(w, b):
        if w == 3:
            return wob.at[b]
        return wqkv.at[w, pl.ds(pl.multiple_of(b * depth, depth), depth)]

    def w_copy(w, b, way, to):
        ref = w_ref(w, b)
        return remote(ref, ref, w_send.at[w, way, b], w_recv.at[w, b], to, t)

    def w_start(w):
        ref, mine = w_own(w), w_ref(w, s)
        for way, to, on in ((2, o * 2 + 1 - i, None), (0, s + 2, o < outer - 1), (1, s - 2, o > 0)):
            def go(way=way, to=to):
                remote(ref, mine, w_send.at[w, way, s], w_recv.at[w, s], to, t).start()
            when(on, go)
        pltpu.make_async_copy(ref, mine, l_sem.at[w]).start()

    def w_step(w, n):
        low, high = s - 2 * n, s + 2 * n

        @pl.when(o - n >= 0)
        def _():
            w_copy(w, low, 0, s).wait_recv()
            pl.when(o < outer - 1)(lambda: w_copy(w, low, 0, s + 2).start())
            w_copy(w, low, 2, o * 2 + 1 - i).start()

        @pl.when(o + n < outer)
        def _():
            w_copy(w, high, 0, s).wait_recv()
            pl.when(o > 0)(lambda: w_copy(w, high, 1, s - 2).start())
            w_copy(w, high, 2, o * 2 + 1 - i).start()

    def w_finish(w):
        for b in range(outer):
            w_copy(w, b * 2 + 1 - i, 0, s).wait_recv()
        pltpu.make_async_copy(w_own(w), w_ref(w, s), l_sem.at[w]).wait()

    def w_end(w):
        for b in range(outer):
            blk = b * 2 + i
            w_copy(w, blk, 2, s).wait_send()
            pl.when((o < outer - 1) & (b <= o))(lambda blk=blk: w_copy(w, blk, 0, s).wait_send())
            pl.when((o > 0) & (b >= o))(lambda blk=blk: w_copy(w, blk, 1, s).wait_send())

    def halo_copy(down):
        if down:
            return remote(state.at[pl.ds(0, HALF)], rows.at[pl.ds(HALF + tok, HALF), cols],
                          h_send.at[1], h_recv.at[1], s - 1, t)
        return remote(state.at[pl.ds(tok - HALF, HALF)], rows.at[pl.ds(0, HALF), cols],
                      h_send.at[0], h_recv.at[0], s + 1, t)

    def mem_copy(src, d, to):
        ref = rows.at[pl.ds(pl.multiple_of(base_slot + src * srows, srows), srows), cols]
        return remote(memory, ref, m_send.at[d], m_recv.at[src], to, t)

    for p in range(nch):
        def tok_copy(lane, to, p=p):
            return remote(state.at[pl.ds(p * CHUNK, CHUNK)], piece_ref(p, t),
                          s_send.at[p, lane], s_recv.at[p, t], s, to)
        for d in range(1, X):
            tok_copy(d, ((x + d) % X) * 2 + c).start()
    for p in range(nch):
        def tok_copy(lane, to, p=p):
            return remote(state.at[pl.ds(p * CHUNK, CHUNK)], piece_ref(p, t),
                          s_send.at[p, lane], s_recv.at[p, t], s, to)
        tok_copy(0, mate).start()
    for d in range(1, n_seq):
        mem_copy(s, d, (s + d) % n_seq).start()
    pl.when(s < n_seq - 1)(lambda: halo_copy(False).start())
    pl.when(s > 0)(lambda: halo_copy(True).start())
    w_start(0)
    rows[pl.ds(HALF, tok), cols] = state[...]
    rows[pl.ds(pl.multiple_of(base_slot + s * srows, srows), srows), cols] = memory[...]

    @pl.when(s == 0)
    def _():
        rows[pl.ds(0, HALF), :] = jnp.zeros((HALF, D), BF16)

    @pl.when(s == n_seq - 1)
    def _():
        rows[pl.ds(HALF + tok, HALF), :] = jnp.zeros((HALF, D), BF16)

    for d in range(1, n_seq):
        mem_copy((s + d) % n_seq, 0, s).wait_recv()
    piece_out(SLOTS)
    pl.when(s > 0)(lambda: halo_copy(False).wait_recv())
    piece_out(BEFORE)
    pl.when(s < n_seq - 1)(lambda: halo_copy(True).wait_recv())
    piece_out(AFTER)
    w_step(0, 1)
    w_start(1)
    piece_forward(0)
    piece_forward(1)
    for n in range(2, outer):
        w_step(0, n)
    for p in range(2, nch):
        piece_forward(p)
    piece_forward(SLOTS)
    piece_forward(BEFORE)
    piece_forward(AFTER)
    w_step(1, 1)
    w_start(2)
    for p in range(nch + 3):
        piece_in(p)
    w_finish(0)

    def project(w, dst, row, size, at):
        dst[pl.ds(at, size), :] = jnp.dot(
            rows[pl.ds(row, size), :], wqkv[w], preferred_element_type=F32
        ).astype(BF16)

    kv_rows = [(r * 2 * CHUNK, 2 * CHUNK) for r in range(base_slot // (2 * CHUNK))] + [(base_slot, slots)]
    q_rows = [(HALF + r * 2 * CHUNK, 2 * CHUNK) for r in range(tok // (2 * CHUNK))] + [(base_slot, slots)]

    def kv_project(w, dst, later, upto):
        for at, (row, size) in enumerate(kv_rows):
            project(w, dst, row, size, row)
            n = at + 2
            if n < outer:
                w_step(later, n)
        for n in range(len(kv_rows) + 2, outer):
            w_step(later, n)

    kv_project(0, k, 1, outer)
    w_step(2, 1)
    w_start(3)
    w_finish(1)
    kv_project(1, v, 2, outer)
    w_step(3, 1)
    w_finish(2)
    project(2, q, base_slot, slots, tok)
    for row, size in q_rows[:-1]:
        project(2, q, row, size, row - HALF)

    place = s.astype(F32)
    gap_row = jnp.abs(homes[...].astype(F32) - place)
    gap_col = jnp.transpose(jnp.broadcast_to(gap_row, (128, slots)))[:, 0:1]

    def slope(h, shape):
        order = jnp.full(shape, (t * heads + h).astype(F32), F32)
        return 0.25 * jnp.exp(order * (math.log(8.0) / (H - 1)))

    nt = (((1,), (1,)), ((), ()))
    lane = lax.broadcasted_iota(jnp.int32, (slots, 128), 1)
    packed = jnp.zeros((slots, 128), F32)
    for h in range(heads):
        hc = slice(h * HD, (h + 1) * HD)
        sc = lax.dot_general(q[pl.ds(tok, slots), hc], k[pl.ds(HALF, tok), hc], nt, preferred_element_type=F32)
        sc = sc * scale - slope(h, (slots, 1)) * gap_col
        top = jnp.max(sc, axis=1, keepdims=True)
        e = jnp.exp(sc - top)
        tot = jnp.sum(e, axis=1, keepdims=True)
        num[:, hc] = jnp.dot(e.astype(BF16), v[pl.ds(HALF, tok), hc], preferred_element_type=F32)
        packed = jnp.where(lane == h, top, packed)
        packed = jnp.where(lane == heads + h, tot, packed)
    stat[...] = packed

    def part_copy(which, src, d, to):
        a, b = ((num, numr), (stat, statr))[which]
        return remote(a.at[pl.ds(pl.multiple_of(to * srows, srows), srows)], b.at[src],
                      p_send.at[which, d], p_recv.at[which, src], to, t)

    for d in range(1, n_seq):
        for which in range(2):
            part_copy(which, s, d, (s + d) % n_seq).start()
    mine = pl.ds(pl.multiple_of(s * srows, srows), srows)
    numr[s] = num[mine, :]
    statr[s] = stat[mine, :]

    span = CHUNK + 2 * HALF

    def attend(j, carry):
        qq = lax.broadcasted_iota(jnp.int32, (CHUNK, span), 0)
        kk = lax.broadcasted_iota(jnp.int32, (CHUNK, span), 1)
        kpos = s * tok + j * CHUNK - HALF + kk
        ok = (kk >= qq) & (kk - qq <= 2 * HALF) & (kpos >= 0) & (kpos < tok * n_seq)
        mask[...] = jnp.where(ok, 0.0, MASKED)
        row = pl.multiple_of(j * CHUNK, CHUNK)
        for h in range(heads):
            hc = slice(h * HD, (h + 1) * HD)
            qh = q[pl.ds(row, CHUNK), hc]
            near = lax.dot_general(qh, k[pl.ds(row, span), hc], nt, preferred_element_type=F32)
            near = near * scale + mask[...]
            far = lax.dot_general(qh, k[pl.ds(base_slot, slots), hc], nt, preferred_element_type=F32)
            far = far * scale - slope(h, (1, slots)) * gap_row
            top = jnp.maximum(jnp.max(near, axis=1, keepdims=True), jnp.max(far, axis=1, keepdims=True))
            en = jnp.exp(near - top)
            ef = jnp.exp(far - top)
            tot = jnp.sum(en, axis=1, keepdims=True) + jnp.sum(ef, axis=1, keepdims=True)
            acc = jnp.dot(en.astype(BF16), v[pl.ds(row, span), hc], preferred_element_type=F32)
            acc = acc + jnp.dot(ef.astype(BF16), v[pl.ds(base_slot, slots), hc], preferred_element_type=F32)
            mixed[pl.ds(row, CHUNK), hc] = (acc / tot).astype(BF16)
        pl.when(j + 2 < outer)(lambda: w_step(3, j + 2))
        return carry

    lax.fori_loop(0, nch, attend, 0)
    for n in range(nch + 2, outer):
        w_step(3, n)

    for d in range(1, n_seq):
        for which in range(2):
            part_copy(which, (s + d) % n_seq, 0, s).wait_recv()
    for h in range(heads):
        hc = slice(h * HD, (h + 1) * HD)
        best = statr[0][:, h:h + 1]
        for b in range(1, n_seq):
            best = jnp.maximum(best, statr[b][:, h:h + 1])
        den = jnp.zeros((srows, 1), F32)
        acc = jnp.zeros((srows, HD), F32)
        for b in range(n_seq):
            weight = jnp.exp(statr[b][:, h:h + 1] - best)
            den = den + weight * statr[b][:, heads + h:heads + h + 1]
            acc = acc + weight * numr[b, :, hc]
        mixed[pl.ds(tok, srows), hc] = (acc / den).astype(BF16)
    w_finish(3)

    nb = width // bw
    outs = [(r * CHUNK, CHUNK) for r in range(nch)] + [(tok, srows)]

    def out_part(r, xd, core):
        row, size = outs[r]
        dest = xd * 2 + core
        a = mixed[pl.ds(row, size), :]
        return [jnp.dot(a, wob[dest * nb + b], preferred_element_type=F32).astype(BF16) for b in range(nb)]

    def core_copy(r, d):
        row, size = outs[r]
        return remote(tosend.at[d, pl.ds(row, size)], pr.at[d, pl.ds(row, size)],
                      c_send.at[r, d], c_recv.at[r, d], s, mate)

    def chip_copy(r, d):
        row, size = outs[r]
        return remote(xsend.at[d, pl.ds(row, size)], xr.at[d, pl.ds(row, size)],
                      x_send.at[r, d], x_recv.at[r, d], s, ((x + d) % X) * 2 + c)

    def store_parts(dst, d, r, parts):
        row, size = outs[r]
        for b, part in enumerate(parts):
            dst[d, pl.ds(row, size), b * bw:(b + 1) * bw] = part

    order = list(range(1, X)) + [0]
    for r in range(len(outs)):
        for d in order:
            store_parts(tosend, d, r, out_part(r, (x + d) % X, 1 - c))
            core_copy(r, d).start()
        for d in order:
            store_parts(xsend, d, r, out_part(r, (x + d) % X, c))
        row, size = outs[r]
        for d in range(1, X):
            core_copy(r, d).wait_recv()
            here = pl.ds(row, size)
            xsend[d, here, :] = (xsend[d, here, :].astype(F32) + pr[d, here, :].astype(F32)).astype(BF16)
            chip_copy(r, d).start()

    def sq_copy(r, d, owner, to):
        if r < nch:
            a, b = sqs.at[r], sqr.at[owner, r]
        else:
            a, b = sqms, sqmr.at[owner]
        return remote(a, b, q_send.at[r, d], q_recv.at[r, owner], s, to)

    for r, (row, size) in enumerate(outs):
        here = pl.ds(row, size)
        core_copy(r, 0).wait_recv()
        total = xsend[0, here, :].astype(F32) + pr[0, here, :].astype(F32)
        for d in range(1, X):
            chip_copy(r, d).wait_recv()
            total = total + xr[d, here, :].astype(F32)
        base = state[here, :] if r < nch else memory[...]
        total = base.astype(F32) + total
        res[here, :] = total
        sq = jnp.broadcast_to(jnp.sum(total * total, axis=1, keepdims=True), (size, 128))
        if r < nch:
            sqs[r] = jnp.transpose(sq)[0:8, :]
            sqr[t, r] = sqs[r]
        else:
            sqms[...] = sq
            sqmr[t] = sq
        for d in range(1, n_tensor):
            sq_copy(r, d, t, (t + d) % n_tensor).start()

    for r, (row, size) in enumerate(outs):
        here = pl.ds(row, size)
        for d in range(1, n_tensor):
            sq_copy(r, 0, (t + d) % n_tensor, t).wait_recv()
        if r < nch:
            sq = sqr[0, r]
            for b in range(1, n_tensor):
                sq = sq + sqr[b, r]
            sq = jnp.transpose(jnp.broadcast_to(sq[0:1, :], (128, size)))[:, 0:1]
        else:
            sq = sqmr[0]
            for b in range(1, n_tensor):
                sq = sq + sqmr[b]
            sq = sq[:, 0:1]
        out = (res[here, :] * lax.rsqrt(sq / D + EPS) * gain[...]).astype(BF16)
        if r < nch:
            left = jnp.broadcast_to(remaining[r:r + 1, :].astype(F32), (128, size))
            live = jnp.transpose(left)[:, 0:1] > 0.5
            new_state[here, :] = jnp.where(live, out.astype(F32), state[here, :].astype(F32)).astype(BF16)
        else:
            new_memory[...] = out

    for w in range(4):
        w_end(w)
    for p in range(nch + 3):
        piece_end(p)
    pl.when(s < n_seq - 1)(lambda: halo_copy(False).wait_send())
    pl.when(s > 0)(lambda: halo_copy(True).wait_send())
    for d in range(1, n_seq):
        mem_copy(s, d, (s + d) % n_seq).wait_send()
        for which in range(2):
            part_copy(which, s, d, (s + d) % n_seq).wait_send()
    for r in range(len(outs)):
        for d in range(X):
            core_copy(r, d).wait_send()
            if d:
                chip_copy(r, d).wait_send()
        for d in range(1, n_tensor):
            sq_copy(r, d, t, (t + d) % n_tensor).wait_send()


def shards(state, memory, w_query, w_key, w_value, w_output, norm_gain, remaining, slot_home):
    n_seq, n_tensor = lax.axis_size("seq"), lax.axis_size("tensor")
    tok, width = state.shape
    srows = memory.shape[0]
    slots = slot_home.shape[0]
    D = width * n_tensor
    X = n_tensor // 2
    nch = tok // CHUNK
    bw = w_output.shape[1]
    R = tok + 2 * HALF + slots
    dma = pltpu.SemaphoreType.DMA
    V = pltpu.VMEM
    return pl.pallas_call(
        functools.partial(kernel, n_seq, n_tensor),
        out_shape=(jax.ShapeDtypeStruct(state.shape, BF16), jax.ShapeDtypeStruct(memory.shape, BF16)),
        in_specs=[pl.BlockSpec(memory_space=V)] * 9,
        out_specs=(pl.BlockSpec(memory_space=V),) * 2,
        scratch_shapes=[
            V((R, D), BF16), V((3, D, width), BF16), V((n_seq, width, bw), BF16),
            V((tok + slots, width), BF16), V((R, width), BF16), V((R, width), BF16),
            V((CHUNK, CHUNK + 2 * HALF), F32), V((tok + srows, width), BF16),
            V((slots, width), F32), V((slots, 128), F32),
            V((n_seq, srows, width), F32), V((n_seq, srows, 128), F32),
            V((X, tok + srows, width), BF16), V((X, tok + srows, width), BF16), V((8, 128), BF16),
            V((X, tok + srows, width), BF16), V((X, tok + srows, width), BF16),
            V((tok + srows, width), F32),
            V((nch, 8, CHUNK), F32), V((n_tensor, nch, 8, CHUNK), F32),
            V((srows, 128), F32), V((n_tensor, srows, 128), F32),
            dma((4, 3, n_seq)), dma((4, n_seq)),
            dma((nch + 3, 2 * X - 1)), dma((nch + 3, n_tensor)),
            dma((2,)), dma((2,)), dma((n_seq,)), dma((n_seq,)), dma((4,)),
            dma((2, n_seq)), dma((2, n_seq)),
            dma((nch + 1, X)), dma((nch + 1, X)), dma((nch + 1, X)), dma((nch + 1, X)),
            dma((nch + 1, n_tensor)), dma((nch + 1, n_tensor)),
        ],
        compiler_params=pltpu.CompilerParams(
            collective_id=0, has_side_effects=True, vmem_limit_bytes=60 * 1024 * 1024
        ),
        cost_estimate=pl.CostEstimate(flops=12_000_000_000, bytes_accessed=8_000_000, transcendentals=4_000_000),
    )(
        state, memory, w_query, w_key, w_value, w_output,
        norm_gain.reshape(1, width), remaining.reshape(nch, CHUNK), slot_home.reshape(1, slots),
    )


def solution(mesh):
    placed = (
        P("seq", "tensor"), P("seq", "tensor"), P("seq", "tensor"), P("seq", "tensor"),
        P("seq", "tensor"), P("tensor", "seq"), P("tensor"), P("seq"), P(),
    )
    return jax.shard_map(
        shards, mesh=mesh, in_specs=placed,
        out_specs=(P("seq", "tensor"), P("seq", "tensor")), check_vma=False,
    )
```

time: 396 us -> 154 us (0.39)
  waiting for transfers between devices: 174 us -> 0 us
  Pallas kernels: 0 us -> 149 us
  blocking collectives: 114 us -> 0 us
  matrix products: 34.8 us -> 0 us
  other arithmetic: 26.5 us -> 0 us
  local copies, waits for them, and re-layouts: 25.6 us -> 4.16 us
  between operations: 14.3 us -> 0.65 us
  starting transfers between devices: 4.83 us -> 0 us
    pallas_call x0 -> x1, Pallas kernels: none -> 149 us  [shards(): pl.pallas_call(functools.partial(kernel, n_seq, n_tensor), out_shape=(jax...]
    all_gather x6 -> x0, waiting for transfers between devices: 130 us -> none  [the longest x1 43.8 us: shards(): lax.all_gather(w_query, 'seq', axis=0, tiled=True)]
    all_gather x4 -> x0, blocking collectives: 108 us -> none  [the longest x2 69.3 us: merged(): gathered = jax.tree.map(lambda a: lax.all_gather(a, axis), part)]
    reduce_scatter x1 -> x0, waiting for transfers between devices: 41.8 us -> none  [shards(): lax.psum_scatter(partial_rows.astype(jnp.bfloat16), 'tensor', scatter_dim...]
    dot_general x14 -> x0, matrix products: 34.8 us -> none  [the longest x3 17.9 us: shards(): jnp.dot(rows_full, piece, preferred_element_type=jnp.float32)]
    concatenate x1 -> x0, other arithmetic: 7.82 us -> none  [with_halo(): array = jnp.concatenate([before, array, after], axis=dim)]
    reduce_sum x4 -> x0, other arithmetic: 7.72 us -> none  [the longest x2 3.69 us: one_block(): total = jnp.sum(exponent_terms, axis=2)]
    psum x1 -> x0, blocking collectives: 5.86 us -> none  [shards(): squares = lax.psum(jnp.sum(residual * residual, axis=1), 'tensor')]
  transfers between devices with their start and end apart: 9 -> 0, of which waited for: 4 -> 0; matrix products, arithmetic and copies ran while one was open for 16% -> 0% of each run, Pallas kernels for 0% -> 0%
where the time goes in v1:
time: 154 us
  Pallas kernels  149 us (97%)
  local copies, waits for them, and re-layouts  4.16 us (3%)
    pallas_call x1, Pallas kernels, shards(): pl.pallas_call(functools.partial(kernel, n_seq, n_tensor), out_shape=(jax...  149 us

profile of v1, /device:TPU:0, one launch (start us, length us, event | category | flops | bytes accessed | tf_op | source)
XLA Modules:
  0.0 154.2 jit_solution(16728892686948878506)
XLA Ops:
  0.6 1.3 reshape.14.remaining
  1.9 149.4 %shard_map.104 = (bf16[1024,512]{1,0:T(8,128)(2,1)}, bf16[16,512]{1,0:T(8,128)(2,1)}) custom-call(bf16[1024,512]{1,0:T(8,128)(2,1)} %state.1, bf16[16,512]{1,0:T(8,128)(2,1)} %memory.1, bf16[256,512]{1,0:T(8,128)(2,1)} %wq.1, bf16[256,512]{1,0:T(8,128)(2,1)} %wk.1, bf16[256,512]{1,0:T(8,128)(2,1)} %wv.1, bf16[512,256]{1,0:T(8,128)(2,1)} %wo.1, ...), custom_call_target="tpu_custom_call" | custom-call | flops 12000000000 | bytes 8000000 | tf_op jit(solution)/shard_map/pallas_call | solution.py:452
  151.3 0.0 copy-start
  151.3 2.3 %copy.13 = bf16[1024,512]{1,0:T(8,128)(2,1)} copy(bf16[1024,512]{1,0:T(8,128)(2,1)} %get-tuple-element.4) | data formatting | bytes 2097152
  153.6 0.0 copy-done
  153.6 0.6 copy.14
Async XLA Ops:
  151.3 2.3 %copy-start = (bf16[16,512]{1,0:T(8,128)(2,1)S(1)}, bf16[16,512]{1,0:T(8,128)(2,1)}, u32[]{:S(2)}) copy-start(bf16[16,512]{1,0:T(8,128)(2,1)} %get-tuple-element.5) | copy-start | bytes 49156

commit v2 on v1

--- a/solution.py
+++ b/solution.py
@@ -24,7 +24,7 @@
     new_state, new_memory,
     rows, wqkv, wob, q, k, v, mask, mixed,
     num, stat, numr, statr,
-    tosend, pr, own, xsend, xr, res, sqs, sqr, sqms, sqmr,
+    tosend, pr, xsend, xr, res, sqs, sqr, sqms, sqmr,
     w_send, w_recv, s_send, s_recv, h_send, h_recv, m_send, m_recv, l_sem,
     p_send, p_recv, c_send, c_recv, x_send, x_recv, q_send, q_recv,
 ):
@@ -112,11 +112,16 @@
                 piece_copy(p, t, lane, mate).wait_send()
         when(piece_on(p), go)
 
+    half = width // 2
+    OUT = 6
+
     def w_own(w):
-        return (wk, wv, wq, wo)[w]
+        if w == OUT:
+            return wo
+        return (wk, wv, wq)[w % 3].at[:, pl.ds((w // 3) * half, half)]
 
     def w_ref(w, b):
-        if w == 3:
+        if isinstance(w, int) and w == OUT:
             return wob.at[b]
         return wqkv.at[w, pl.ds(pl.multiple_of(b * depth, depth), depth)]
 
@@ -204,50 +209,59 @@
     piece_out(BEFORE)
     pl.when(s < n_seq - 1)(lambda: halo_copy(True).wait_recv())
     piece_out(AFTER)
-    w_step(0, 1)
-    w_start(1)
+    steps = outer - 1
+    issued = [0, 1]
+
+    def start_upto(w):
+        while issued[1] <= min(w, OUT):
+            w_start(issued[1])
+            issued[1] += 1
+
+    def relay_one():
+        g = issued[0]
+        w, n = g // steps, 1 + g % steps
+        if w > OUT:
+            return
+        start_upto(w)
+        w_step(w, n)
+        issued[0] += 1
+        if n == 1:
+            start_upto(w + 1)
+
+    def relay_upto(w, n):
+        while issued[0] < min(w, OUT + 1) * steps + n and issued[0] < (OUT + 1) * steps:
+            relay_one()
+
+    relay_upto(0, 1)
     piece_forward(0)
     piece_forward(1)
-    for n in range(2, outer):
-        w_step(0, n)
+    relay_upto(1, 0)
     for p in range(2, nch):
         piece_forward(p)
     piece_forward(SLOTS)
     piece_forward(BEFORE)
     piece_forward(AFTER)
-    w_step(1, 1)
-    w_start(2)
+    relay_upto(1, 1)
     for p in range(nch + 3):
         piece_in(p)
-    w_finish(0)
 
     def project(w, dst, row, size, at):
-        dst[pl.ds(at, size), :] = jnp.dot(
+        hc = slice((w // 3) * half, (w // 3 + 1) * half)
+        dst[pl.ds(at, size), hc] = jnp.dot(
             rows[pl.ds(row, size), :], wqkv[w], preferred_element_type=F32
         ).astype(BF16)
 
     kv_rows = [(r * 2 * CHUNK, 2 * CHUNK) for r in range(base_slot // (2 * CHUNK))] + [(base_slot, slots)]
     q_rows = [(HALF + r * 2 * CHUNK, 2 * CHUNK) for r in range(tok // (2 * CHUNK))] + [(base_slot, slots)]
 
-    def kv_project(w, dst, later, upto):
-        for at, (row, size) in enumerate(kv_rows):
-            project(w, dst, row, size, row)
-            n = at + 2
-            if n < outer:
-                w_step(later, n)
-        for n in range(len(kv_rows) + 2, outer):
-            w_step(later, n)
-
-    kv_project(0, k, 1, outer)
-    w_step(2, 1)
-    w_start(3)
-    w_finish(1)
-    kv_project(1, v, 2, outer)
-    w_step(3, 1)
-    w_finish(2)
-    project(2, q, base_slot, slots, tok)
-    for row, size in q_rows[:-1]:
-        project(2, q, row, size, row - HALF)
+    def project_all(w):
+        dst = (k, v, q)[w % 3]
+        relay_upto(w + 1, 1)
+        w_finish(w)
+        for at, (row, size) in enumerate(q_rows if w % 3 == 2 else kv_rows):
+            project(w, dst, row, size, row - HALF if w % 3 == 2 and row < base_slot else (tok if w % 3 == 2 else row))
+            if at < 2 and w + 1 < OUT:
+                relay_upto(w + 1, at + 2)
 
     place = s.astype(F32)
     gap_row = jnp.abs(homes[...].astype(F32) - place)
@@ -259,41 +273,43 @@
 
     nt = (((1,), (1,)), ((), ()))
     lane = lax.broadcasted_iota(jnp.int32, (slots, 128), 1)
-    packed = jnp.zeros((slots, 128), F32)
-    for h in range(heads):
-        hc = slice(h * HD, (h + 1) * HD)
-        sc = lax.dot_general(q[pl.ds(tok, slots), hc], k[pl.ds(HALF, tok), hc], nt, preferred_element_type=F32)
-        sc = sc * scale - slope(h, (slots, 1)) * gap_col
-        top = jnp.max(sc, axis=1, keepdims=True)
-        e = jnp.exp(sc - top)
-        tot = jnp.sum(e, axis=1, keepdims=True)
-        num[:, hc] = jnp.dot(e.astype(BF16), v[pl.ds(HALF, tok), hc], preferred_element_type=F32)
-        packed = jnp.where(lane == h, top, packed)
-        packed = jnp.where(lane == heads + h, tot, packed)
-    stat[...] = packed
+    def slot_heads(which):
+        packed = stat[...] if which else jnp.zeros((slots, 128), F32)
+        for h in range(which * heads // 2, (which + 1) * heads // 2):
+            hc = slice(h * HD, (h + 1) * HD)
+            sc = lax.dot_general(q[pl.ds(tok, slots), hc], k[pl.ds(HALF, tok), hc], nt, preferred_element_type=F32)
+            sc = sc * scale - slope(h, (slots, 1)) * gap_col
+            top = jnp.max(sc, axis=1, keepdims=True)
+            e = jnp.exp(sc - top)
+            tot = jnp.sum(e, axis=1, keepdims=True)
+            num[:, hc] = jnp.dot(e.astype(BF16), v[pl.ds(HALF, tok), hc], preferred_element_type=F32)
+            packed = jnp.where(lane == h, top, packed)
+            packed = jnp.where(lane == heads + h, tot, packed)
+        stat[...] = packed
 
     def part_copy(which, src, d, to):
         a, b = ((num, numr), (stat, statr))[which]
         return remote(a.at[pl.ds(pl.multiple_of(to * srows, srows), srows)], b.at[src],
                       p_send.at[which, d], p_recv.at[which, src], to, t)
 
-    for d in range(1, n_seq):
-        for which in range(2):
-            part_copy(which, s, d, (s + d) % n_seq).start()
-    mine = pl.ds(pl.multiple_of(s * srows, srows), srows)
-    numr[s] = num[mine, :]
-    statr[s] = stat[mine, :]
+    def parts_out():
+        for d in range(1, n_seq):
+            for which in range(2):
+                part_copy(which, s, d, (s + d) % n_seq).start()
+        mine = pl.ds(pl.multiple_of(s * srows, srows), srows)
+        numr[s] = num[mine, :]
+        statr[s] = stat[mine, :]
 
     span = CHUNK + 2 * HALF
 
-    def attend(j, carry):
+    def attend(which, relay, j, carry):
         qq = lax.broadcasted_iota(jnp.int32, (CHUNK, span), 0)
         kk = lax.broadcasted_iota(jnp.int32, (CHUNK, span), 1)
         kpos = s * tok + j * CHUNK - HALF + kk
         ok = (kk >= qq) & (kk - qq <= 2 * HALF) & (kpos >= 0) & (kpos < tok * n_seq)
         mask[...] = jnp.where(ok, 0.0, MASKED)
         row = pl.multiple_of(j * CHUNK, CHUNK)
-        for h in range(heads):
+        for h in range(which * heads // 2, (which + 1) * heads // 2):
             hc = slice(h * HD, (h + 1) * HD)
             qh = q[pl.ds(row, CHUNK), hc]
             near = lax.dot_general(qh, k[pl.ds(row, span), hc], nt, preferred_element_type=F32)
@@ -307,12 +323,37 @@
             acc = jnp.dot(en.astype(BF16), v[pl.ds(row, span), hc], preferred_element_type=F32)
             acc = acc + jnp.dot(ef.astype(BF16), v[pl.ds(base_slot, slots), hc], preferred_element_type=F32)
             mixed[pl.ds(row, CHUNK), hc] = (acc / tot).astype(BF16)
-        pl.when(j + 2 < outer)(lambda: w_step(3, j + 2))
+        relay(j)
         return carry
 
-    lax.fori_loop(0, nch, attend, 0)
-    for n in range(nch + 2, outer):
-        w_step(3, n)
+    for w in range(3):
+        project_all(w)
+    slot_heads(0)
+    relay_upto(4, 1)
+    start_upto(5)
+    first = issued[0]
+
+    def relay_early(j):
+        g = first + j
+        pl.when(g < OUT * steps)(lambda: w_step(g // steps, 1 + g % steps))
+
+    lax.fori_loop(0, nch, functools.partial(attend, 0, relay_early), 0)
+    issued[0] = min(first + nch, OUT * steps)
+    start_upto(OUT)
+    for w in range(3, 6):
+        if w < 5:
+            relay_upto(w + 1, 0)
+        project_all(w)
+    slot_heads(1)
+    parts_out()
+    late = issued[0] - OUT * steps + 1
+
+    def relay_late(j):
+        pl.when(j + late < outer)(lambda: w_step(OUT, j + late))
+
+    lax.fori_loop(0, nch, functools.partial(attend, 1, relay_late), 0)
+    for n in range(nch + late, outer):
+        w_step(OUT, n)
 
     for d in range(1, n_seq):
         for which in range(2):
@@ -329,7 +370,7 @@
             den = den + weight * statr[b][:, heads + h:heads + h + 1]
             acc = acc + weight * numr[b, :, hc]
         mixed[pl.ds(tok, srows), hc] = (acc / den).astype(BF16)
-    w_finish(3)
+    w_finish(OUT)
 
     nb = width // bw
     outs = [(r * CHUNK, CHUNK) for r in range(nch)] + [(tok, srows)]
@@ -418,7 +459,7 @@
         else:
             new_memory[...] = out
 
-    for w in range(4):
+    for w in range(OUT + 1):
         w_end(w)
     for p in range(nch + 3):
         piece_end(p)
@@ -455,19 +496,19 @@
         in_specs=[pl.BlockSpec(memory_space=V)] * 9,
         out_specs=(pl.BlockSpec(memory_space=V),) * 2,
         scratch_shapes=[
-            V((R, D), BF16), V((3, D, width), BF16), V((n_seq, width, bw), BF16),
+            V((R, D), BF16), V((6, D, width // 2), BF16), V((n_seq, width, bw), BF16),
             V((tok + slots, width), BF16), V((R, width), BF16), V((R, width), BF16),
             V((CHUNK, CHUNK + 2 * HALF), F32), V((tok + srows, width), BF16),
             V((slots, width), F32), V((slots, 128), F32),
             V((n_seq, srows, width), F32), V((n_seq, srows, 128), F32),
-            V((X, tok + srows, width), BF16), V((X, tok + srows, width), BF16), V((8, 128), BF16),
+            V((X, tok + srows, width), BF16), V((X, tok + srows, width), BF16),
             V((X, tok + srows, width), BF16), V((X, tok + srows, width), BF16),
             V((tok + srows, width), F32),
             V((nch, 8, CHUNK), F32), V((n_tensor, nch, 8, CHUNK), F32),
             V((srows, 128), F32), V((n_tensor, srows, 128), F32),
-            dma((4, 3, n_seq)), dma((4, n_seq)),
+            dma((7, 3, n_seq)), dma((7, n_seq)),
             dma((nch + 3, 2 * X - 1)), dma((nch + 3, n_tensor)),
-            dma((2,)), dma((2,)), dma((n_seq,)), dma((n_seq,)), dma((4,)),
+            dma((2,)), dma((2,)), dma((n_seq,)), dma((n_seq,)), dma((7,)),
             dma((2, n_seq)), dma((2, n_seq)),
             dma((nch + 1, X)), dma((nch + 1, X)), dma((nch + 1, X)), dma((nch + 1, X)),
             dma((nch + 1, n_tensor)), dma((nch + 1, n_tensor)),

time: 154 us -> 165 us (1.071)
  Pallas kernels: 149 us -> 160 us
    pallas_call x1, Pallas kernels: 149 us -> 160 us  [shards(): pl.pallas_call(functools.partial(kernel, n_seq, n_tensor), out_shape=(jax...]
where the time goes in v2:
time: 165 us
  Pallas kernels  160 us (97%)
  local copies, waits for them, and re-layouts  4.16 us (3%)
    pallas_call x1, Pallas kernels, shards(): pl.pallas_call(functools.partial(kernel, n_seq, n_tensor), out_shape=(jax...  160 us

profile of v2, /device:TPU:0, one launch (start us, length us, event | category | flops | bytes accessed | tf_op | source)
XLA Modules:
  0.0 164.6 jit_solution(5542549326611181760)
XLA Ops:
  0.6 1.3 reshape.14.remaining
  1.9 159.8 %shard_map.104 = (bf16[1024,512]{1,0:T(8,128)(2,1)}, bf16[16,512]{1,0:T(8,128)(2,1)}) custom-call(bf16[1024,512]{1,0:T(8,128)(2,1)} %state.1, bf16[16,512]{1,0:T(8,128)(2,1)} %memory.1, bf16[256,512]{1,0:T(8,128)(2,1)} %wq.1, bf16[256,512]{1,0:T(8,128)(2,1)} %wk.1, bf16[256,512]{1,0:T(8,128)(2,1)} %wv.1, bf16[512,256]{1,0:T(8,128)(2,1)} %wo.1, ...), custom_call_target="tpu_custom_call" | custom-call | flops 12000000000 | bytes 8000000 | tf_op jit(solution)/shard_map/pallas_call | solution.py:493
  161.7 0.0 copy-start
  161.8 2.3 %copy.13 = bf16[1024,512]{1,0:T(8,128)(2,1)} copy(bf16[1024,512]{1,0:T(8,128)(2,1)} %get-tuple-element.4) | data formatting | bytes 2097152
  164.0 0.0 copy-done
  164.0 0.6 copy.14
Async XLA Ops:
  161.7 2.3 %copy-start = (bf16[16,512]{1,0:T(8,128)(2,1)S(1)}, bf16[16,512]{1,0:T(8,128)(2,1)}, u32[]{:S(2)}) copy-start(bf16[16,512]{1,0:T(8,128)(2,1)} %get-tuple-element.5) | copy-start | bytes 49156
